TPU v7x, 128 devices: a whole 4x4x4 slice. The times are simulated.
128 devices in a mesh: worker: 8 (over y, z_hi), fsdp: 16 (over z_lo, x, core).
Axes of the slice: x: 4, y: 4, z: 4 (z_hi: 2, z_lo: 2; z = z_hi * 2 + z_lo), core: 2. Of those that a mesh axis runs over, the one named last changes fastest.
Arguments:
- local_params: float32 [8, 4096, 8192], P('worker', None, 'fsdp'), may hold values from -6 to 6
- global_params: float32 [4096, 8192], P(('worker', 'fsdp')), may hold values from -6 to 6
- momentum: float32 [4096, 8192], P(('worker', 'fsdp')), may hold values from -3 to 3
- step_counts: int32 [8], P('worker'), may hold values from 64 to 256
- alive: int32 [8], P('worker'), may hold values from 0 to 1, as said below
Outputs:
- new_params: float32 [4096, 8192], P(None, 'fsdp')
- new_momentum: float32 [4096, 8192], P(('worker', 'fsdp'))
Inputs may be any that keep to these rules, and one draw needn't show every extreme that they name: Exactly one worker has alive 0.
All inputs are finite; a program needn't handle non-finite values.
Results may differ from a plain program's by a relative error of at most 0.00007.
Values sent between devices are 32-bit elements; how exact they have to be, the bound alone decides.
A program may use at most 128 MiB of HBM per device.

v0:
```python
import jax
import jax.numpy as jnp
from jax import lax
from jax.sharding import PartitionSpec as P


def local(local_params, global_params, momentum, step_counts, alive):
    weight = (step_counts * alive).astype(jnp.float32)
    total = lax.psum(weight, "worker")
    term = weight[0] * local_params[0]
    shared = lax.psum_scatter(term, "worker", scatter_dimension=0, tiled=True)
    summed = lax.all_to_all(shared, "fsdp", split_axis=0, concat_axis=1, tiled=True)
    average = summed / total[0]
    outer_grad = global_params - average
    new_momentum = 0.9 * momentum + outer_grad
    new_global = global_params - 0.7 * (outer_grad + 0.9 * new_momentum)
    pieces = lax.all_to_all(new_global, "fsdp", split_axis=1, concat_axis=0, tiled=True)
    new_params = lax.all_gather(pieces, "worker", axis=0, tiled=True)
    return (new_params, new_momentum)


def solution(mesh):
    in_specs = (
        P("worker", None, "fsdp"),
        P(("worker", "fsdp"), None),
        P(("worker", "fsdp"), None),
        P("worker"),
        P("worker"),
    )
    out_specs = (P(None, "fsdp"), P(("worker", "fsdp"), None))
    return jax.shard_map(local, mesh=mesh, in_specs=in_specs, out_specs=out_specs, check_vma=False)
```

profile of v0, /device:TPU:1, one launch (start us, length us, event | category | flops | bytes accessed | tf_op | source)
XLA Modules:
  0.0 308.5 jit_solution(16416931315925339776)
XLA Ops:
  7.2 0.0 reduce-scatter.2.cloned.1.call-start
  8.5 7.8 %multiply_bitcast_fusion = f32[4096,512]{1,0:T(8,128)} fusion(f32[1,4096,512]{2,1,0:T(8,128)} %param.5, f32[]{:T(128)} %bitcast), kind=kLoop, calls=%fused_computation | loop fusion | flops 2097152 | bytes 16777220 | tf_op jit(solution)/shard_map/mul | solution.py:10
  16.3 0.0 copy-start
  16.3 0.0 copy-start.1
  16.3 0.0 reduce-scatter.2.cloned.1.call-update
  16.3 117.2 %reduce-scatter.2.cloned.1.call-done = f32[512,512]{1,0:T(8,128)} async-done(((f32[4096,512]{1,0:T(8,128)}), f32[512,512]{1,0:T(8,128)}) %reduce-scatter.2.cloned.1.call-update) | async-done | bytes 1048592 | tf_op jit(solution)/shard_map/reduce_scatter | solution.py:11
  133.5 5.6 %all-to-all-start = ((f32[16,32,512]{2,1,0:T(8,128)}), f32[16,32,512]{2,1,0:T(8,128)S(1)}, u32[]{:S(2)}, u32[]{:S(2)}) async-start(f32[16,32,512]{2,1,0:T(8,128)} %bitcast.19), calls=%async_computation.1 | async-start | bytes 2097152 | tf_op jit(solution)/shard_map/all_to_all | solution.py:12
  139.1 0.0 all-gather.2.cloned.1.call-start
  139.2 19.9 %psum.7 = f32[]{:T(128)} all-reduce(f32[]{:T(128)} %bitcast), channel_id=1, replica_groups=mesh['worker'=8,'fsdp'=16] {'worker'}, use_global_device_ids=true, to_apply=%region_1.0 | all-reduce | flops 1 | bytes 8 | tf_op jit(solution)/shard_map/psum | solution.py:9
  159.1 0.0 all-to-all-done
  159.1 0.8 divide_bitcast_fusion
  159.9 0.1 copy.12
  160.0 0.0 copy-done
  160.0 0.0 copy-done.1
  160.0 1.2 multiply_subtract_fusion
  161.2 0.1 copy.14
  161.3 28.7 %all_to_all.32 = f32[32,16,512]{2,0,1:T(8,128)} all-to-all(f32[32,16,512]{2,0,1:T(8,128)S(1)} %bitcast.18), channel_id=1, replica_groups=mesh['worker'=8,'fsdp'=16] {'fsdp'}, dimensions={1} | all-to-all | bytes 2097152 | tf_op jit(solution)/shard_map/all_to_all | solution.py:17
  190.1 0.0 all-gather.2.cloned.1.call-update
  190.1 103.9 %all-gather.2.cloned.1.call-done = f32[4096,512]{1,0:T(8,128)} async-done(((f32[512,512]{1,0:T(8,128)}), f32[4096,512]{1,0:T(8,128)}) %all-gather.2.cloned.1.call-update) | async-done | bytes 8388624 | tf_op jit(solution)/shard_map/all_gather | solution.py:18
  293.9 7.8 %copy.18 = f32[4096,512]{1,0:T(8,128)} copy(f32[4096,512]{1,0:T(8,128)} %all-gather.2.cloned.1.call-done) | data formatting | bytes 16777216
Async XLA Ops:
  7.2 126.3 %reduce-scatter.2.cloned.1.call-start = ((), (), s32[]{:S(2)}) async-start(), calls=%async_computation.3 | async-start | bytes 9437184 | tf_op jit(solution)/shard_map/reduce_scatter | solution.py:11
  16.3 143.7 %copy-start = (f32[32,8192]{1,0:T(8,128)S(1)}, f32[32,8192]{1,0:T(8,128)}, u32[]{:S(2)}) copy-start(f32[32,8192]{1,0:T(8,128)} %param.6) | copy-start | bytes 3145732
  16.3 143.7 %copy-start.1 = (f32[32,8192]{1,0:T(8,128)S(1)}, f32[32,8192]{1,0:T(8,128)}, u32[]{:S(2)}) copy-start(f32[32,8192]{1,0:T(8,128)} %param.7) | copy-start | bytes 3145732
  133.5 25.6 %all-to-all-start = ((f32[16,32,512]{2,1,0:T(8,128)}), f32[16,32,512]{2,1,0:T(8,128)S(1)}, u32[]{:S(2)}, u32[]{:S(2)}) async-start(f32[16,32,512]{2,1,0:T(8,128)} %bitcast.19), calls=%async_computation.1 | async-start | bytes 2097152 | tf_op jit(solution)/shard_map/all_to_all | solution.py:12
  139.1 154.8 %all-gather.2.cloned.1.call-start = ((), (), s32[]{:S(2)}) async-start(), calls=%async_computation.4 | async-start | bytes 9437184 | tf_op jit(solution)/shard_map/all_gather | solution.py:18
Sparse Core Ops, SparseCore 0:
  16.5 116.9 reduce-scatter.1
  190.2 103.6 all-gather.1
where the time goes:
time: 309 us
  waiting for transfers between devices  221 us (72%)
  blocking collectives  48.7 us (16%)
  between operations  15.4 us (5%)
  other arithmetic  9.84 us (3%)
  local copies, waits for them, and re-layouts  7.9 us (3%)
  starting transfers between devices  5.68 us (2%)
    reduce_scatter x1, waiting for transfers between devices, local(): shared = lax.psum_scatter(term, 'worker', scatter_dimension=0, tiled=True)  117 us
    all_gather x1, waiting for transfers between devices, local(): new_params = lax.all_gather(pieces, 'worker', axis=0, tiled=True)  104 us
    all_to_all x1, blocking collectives, local(): lax.all_to_all(new_global, 'fsdp', split_axis=1, concat_axis=0, tiled=True)  28.7 us
    psum x1, blocking collectives, local(): total = lax.psum(weight, 'worker')  19.9 us
    mul x1, other arithmetic, local(): term = weight[0] * local_params[0]  7.81 us
    unnamed x5, local copies, waits for them, and re-layouts  7.76 us
  transfers between devices with their start and end apart: 3, of which 2 were waited for; matrix products, arithmetic and copies ran while one was open for 0% of the time, Pallas kernels for 0%

commit v1 on v0

v1 whole, which is shorter than its diff:
```python
import functools

import jax
import jax.numpy as jnp
from jax import lax
from jax.experimental import pallas as pl
from jax.experimental.pallas import tpu as pltpu
from jax.sharding import PartitionSpec as P

MESH = pl.DeviceIdType.MESH
F32 = jnp.float32

A = (64, 64, 64, 64, 64, 32,)
B = (64, 64, 32,)
ORDER = [(c[0], c[1], int(c[2])) for c in (
    "LA0", "LB0", "LA1", "CA0", "FB0", "LB1", "LA2", "CA1", "ZA0", "CB0", "CA2", "LB2",
    "ZA1", "LA3", "FB1", "H00", "LA4", "LA5", "ZA2", "FB2", "CA3", "CA4", "CA5", "ZA3",
    "CB1", "NB0", "ZA4", "NA0", "ZA5", "NA1", "NB1", "XB0", "PA0", "CB2", "PA1", "XB1",
    "XA0", "YB0", "XA1", "YA0", "NB2", "NA2", "YB1", "YA1", "NA3", "EB0", "EA0", "XB2",
    "PA2", "XA2", "EA1", "NA4", "EB1", "NA5", "YB2", "PA3", "V00", "YA2", "XA3", "PA4",
    "EB2", "PA5", "XA4", "YA3", "EA2", "XA5", "YA4", "YA5", "M00", "EA3", "EA4", "EA5",
)]


def pieces():
    at, out = 0, {}
    for kind, sizes in (("A", A), ("B", B)):
        for p, n in enumerate(sizes):
            out[kind, p] = (at, n)
            at += n
    return out


PIECES = pieces()
TAGS = {
    "A": ("fr", "fl", "cr", "cl", "z", "gz", "gr", "gl", "pr", "pl", "xr", "xl", "yr", "yl"),
    "B": ("zb0", "zb1", "zb2", "zb3", "fr", "fl", "cr", "cl", "gr", "gl", "xr", "xl", "gz0", "gz1", "gz2", "gz3"),
}
INDEX = {key: i for i, key in enumerate((t, k, p) for (k, p) in PIECES for t in TAGS[k])}


def kernel(
    local_ref, g_hbm, m_hbm, steps_ref, alive_ref, out, nm_out,
    work, rf, rcl, rcr, rz, g, m, hs, hr, av, avr, wt, inv,
    load_sem, gm_sem, send_sem, recv_sem, wt_send, wt_recv, h_send, h_recv, v_send, v_recv,
):
    w, f = lax.axis_index("worker"), lax.axis_index("fsdp")
    y, zh = w // 2, w % 2
    zo = 1 - zh
    yr, yl, y2 = (y + 1) % 4, (y + 3) % 4, (y + 2) % 4
    right, left, over = (yr * 2 + zh, f), (yl * 2 + zh, f), (y * 2 + zo, f)

    def load(key):
        at, n = PIECES[key]
        rows = pl.ds(at, n)
        i = list(PIECES).index(key)
        return pltpu.make_async_copy(local_ref.at[:, :, rows], work.at[:, :, rows], load_sem.at[i])

    lorder = [(k, p) for s, k, p in ORDER if s == "L"]
    for key in lorder[:2]:
        load(key).start()
    g_copy = pltpu.make_async_copy(g_hbm, g, gm_sem.at[0])
    m_copy = pltpu.make_async_copy(m_hbm, m, gm_sem.at[1])
    g_copy.start()
    m_copy.start()
    for key in lorder[2:]:
        load(key).start()

    barrier = pltpu.get_barrier_semaphore()

    def greet_worker(d, c):
        pl.semaphore_signal(barrier, inc=1, device_id=((w + d) % 8, f), device_id_type=MESH)
        return c

    def greet_fsdp(d, c):
        pl.semaphore_signal(barrier, inc=1, device_id=(w, (f + d) % 16), device_id_type=MESH)
        return c

    lax.fori_loop(1, 8, greet_worker, 0)
    lax.fori_loop(1, 16, greet_fsdp, 0)

    weight = (steps_ref[0] * alive_ref[0]).astype(F32)

    def channel(tag, kind, p):
        at, n = PIECES[kind, p]
        half = n // 2
        rows, lo, hi = pl.ds(at, n), pl.ds(at, half), pl.ds(at + half, half)
        if tag[:2] == "zb":
            t = {"0": y, "1": yr, "2": y2, "3": yl}[tag[2]]
            return work.at[t, zo, rows], rz.at[t, rows], over, rz.at[t, rows]
        if tag == "z":
            return work.at[y, zo, rows], rz.at[0, rows], over, rz.at[0, rows]
        if tag in ("fr", "fl", "cr", "cl"):
            z, q = (slice(None), slice(None)) if kind == "A" else (zh, 0)
            if tag == "fr":
                return work.at[y2, z, lo], rf.at[q, lo], right, rf.at[q, lo]
            if tag == "fl":
                return work.at[y2, z, hi], rf.at[q, hi], left, rf.at[q, hi]
            if tag == "cr":
                return work.at[yr, z, rows], rcl.at[q, rows], right, rcl.at[q, rows]
            return work.at[yl, z, rows], rcr.at[q, rows], left, rcr.at[q, rows]
        if tag[:2] == "gz":
            t = {"": y, "0": y, "1": yl, "2": y2, "3": yr}[tag[2:]]
            return out.at[t, zh, rows], out.at[t, zh, rows], over, out.at[t, zo, rows]
        z = zo if tag[0] in "py" else zh
        if tag in ("gr", "pr"):
            return out.at[y, z, rows], out.at[y, z, rows], right, out.at[yl, z, rows]
        if tag in ("gl", "pl"):
            return out.at[y, z, rows], out.at[y, z, rows], left, out.at[yr, z, rows]
        if tag in ("xr", "yr"):
            return out.at[yl, z, lo], out.at[yl, z, lo], right, out.at[y2, z, lo]
        return out.at[yr, z, hi], out.at[yr, z, hi], left, out.at[y2, z, hi]

    sent = []

    def send(tag, kind, p):
        src, dst, device, _ = channel(tag, kind, p)
        i = INDEX[tag, kind, p]
        copy = pltpu.make_async_remote_copy(
            src, dst, send_sem.at[i], recv_sem.at[i], device_id=device, device_id_type=MESH
        )
        copy.start()
        sent.append(copy)

    def wait(tag, kind, p):
        src, _, device, land = channel(tag, kind, p)
        i = INDEX[tag, kind, p]
        pltpu.make_async_remote_copy(
            src, land, send_sem.at[i], recv_sem.at[i], device_id=device, device_id_type=MESH
        ).wait_recv()

    def weigh(key):
        at, n = PIECES[key]
        load(key).wait()

        def body(i, c):
            ref = work.at[i // 2, i % 2, pl.ds(at, n)]
            ref[...] = ref[...] * weight
            return c

        lax.fori_loop(0, 8, body, 0)

    def wt_copy(d):
        to, source = (w + d) % 8, (w + 8 - d) % 8
        return pltpu.make_async_remote_copy(
            wt.at[w], wt.at[w], wt_send.at[d], wt_recv.at[d], device_id=(to, f), device_id_type=MESH
        ), pltpu.make_async_remote_copy(
            wt.at[w], wt.at[source], wt_send.at[d], wt_recv.at[d], device_id=(to, f), device_id_type=MESH
        )

    def h_copy(d):
        to, source = (f + d) % 16, (f + 16 - d) % 16
        dst = hr.at[pl.ds(pl.multiple_of(32 * f, 32), 32)]
        land = hr.at[pl.ds(pl.multiple_of(32 * source, 32), 32)]
        return tuple(
            pltpu.make_async_remote_copy(
                hs.at[to], t, h_send.at[d], h_recv.at[d], device_id=(w, to), device_id_type=MESH
            )
            for t in (dst, land)
        )

    def v_copy(d):
        to, source = (f + d) % 16, (f + 16 - d) % 16
        src = av.at[pl.ds(pl.multiple_of(32 * to, 32), 32)]
        return tuple(
            pltpu.make_async_remote_copy(
                src, t, v_send.at[d], v_recv.at[d], device_id=(w, to), device_id_type=MESH
            )
            for t in (avr.at[f], avr.at[source])
        )

    def each(copies, n, what):
        def body(d, c):
            out_copy, in_copy = copies(d)
            if what == "start":
                out_copy.start()
            elif what == "recv":
                in_copy.wait_recv()
            else:
                out_copy.wait_send()
            return c

        lax.fori_loop(1, n, body, 0)

    ready = []

    def need_h():
        if ready:
            return
        ready.append(True)
        each(wt_copy, 8, "recv")
        total = wt[0]
        for i in range(1, 8):
            total = total + wt[i]
        inv[...] = 1.0 / total
        each(h_copy, 16, "recv")

    def finish(at, n, s):
        rows = pl.ds(at, n)
        average = s * inv[0:1, :]
        av[rows] = average
        out[y, zh, rows] = 1.33 * average + hr[rows]

    entered = []
    for step, kind, p in ORDER:
        if step == "H":
            g_copy.wait()
            m_copy.wait()
            for i in range(16):
                cols = pl.ds(512 * i, 512)
                hs[i] = -0.33 * g[:, cols] - 0.567 * m[:, cols]
            hr[pl.ds(pl.multiple_of(32 * f, 32), 32)] = hs[f]
            each(h_copy, 16, "start")
            continue
        if step == "V":
            avr[f] = av[pl.ds(pl.multiple_of(32 * f, 32), 32)]
            each(v_copy, 16, "start")
            continue
        if step == "M":
            each(v_copy, 16, "recv")
            for i in range(16):
                cols = pl.ds(512 * i, 512)
                nm_out[:, cols] = 0.9 * m[:, cols] + (g[:, cols] - avr[i])
            continue
        at, n = PIECES[kind, p]
        half = n // 2
        rows, lo, hi = pl.ds(at, n), pl.ds(at, half), pl.ds(at + half, half)
        if step == "L":
            weigh((kind, p))
            if not entered:
                entered.append(True)
                wt[w] = jnp.full((8, 512), weight, F32)
                pl.semaphore_wait(barrier, 22)
                each(wt_copy, 8, "start")
            for tag in ("fr", "fl") if kind == "A" else ("zb2", "zb1", "zb3", "zb0"):
                send(tag, kind, p)
        elif step == "F":
            wait("zb2", kind, p)
            work[y2, zh, rows] += rz[y2, rows]
            send("fr", kind, p)
            send("fl", kind, p)
        elif step == "C":
            wait("fr", kind, p)
            wait("fl", kind, p)
            if kind == "A":
                for z in range(2):
                    work[yr, z, lo] += rf[z, lo]
                    work[yl, z, hi] += rf[z, hi]
            else:
                wait("zb1", kind, p)
                wait("zb3", kind, p)
                work[yr, zh, lo] += rz[yr, lo] + rf[0, lo]
                work[yr, zh, hi] += rz[yr, hi]
                work[yl, zh, lo] += rz[yl, lo]
                work[yl, zh, hi] += rz[yl, hi] + rf[0, hi]
            send("cr", kind, p)
            send("cl", kind, p)
        elif step == "Z":
            wait("cr", kind, p)
            wait("cl", kind, p)
            for z in range(2):
                work[y, z, rows] += rcl[z, rows] + rcr[z, rows]
            send("z", kind, p)
        elif step == "N":
            if kind == "A":
                wait("z", kind, p)
                need_h()
                finish(at, n, work[y, zh, rows] + rz[0, rows])
                for tag in ("gz", "gr", "gl"):
                    send(tag, kind, p)
            else:
                wait("cr", kind, p)
                wait("cl", kind, p)
                wait("zb0", kind, p)
                need_h()
                finish(at, n, work[y, zh, rows] + rz[y, rows] + rcl[0, rows] + rcr[0, rows])
                for tag in ("gr", "gl", "gz0"):
                    send(tag, kind, p)
        elif step == "P":
            wait("gz", kind, p)
            send("pr", kind, p)
            send("pl", kind, p)
        elif step == "X":
            wait("gr", kind, p)
            wait("gl", kind, p)
            send("xr", kind, p)
            send("xl", kind, p)
            if kind == "B":
                send("gz1", kind, p)
                send("gz3", kind, p)
        elif step == "Y":
            if kind == "A":
                wait("pr", kind, p)
                wait("pl", kind, p)
                send("yr", kind, p)
                send("yl", kind, p)
            else:
                wait("xr", kind, p)
                wait("xl", kind, p)
                send("gz2", kind, p)
        elif step == "E":
            for tag in ("xr", "xl", "yr", "yl") if kind == "A" else ("gz0", "gz1", "gz3", "gz2"):
                wait(tag, kind, p)

    for copy in sent:
        copy.wait_send()
    each(wt_copy, 8, "sent")
    each(h_copy, 16, "sent")
    each(v_copy, 16, "sent")


def local(local_params, global_params, momentum, step_counts, alive):
    hbm = pl.BlockSpec(memory_space=pltpu.HBM)
    smem = pl.BlockSpec(memory_space=pltpu.SMEM)
    n = len(INDEX)
    dma = pltpu.SemaphoreType.DMA
    out, nm = pl.pallas_call(
        kernel,
        out_shape=(pltpu.VMEM((4, 2, 512, 512), F32), pltpu.VMEM((32, 8192), F32)),
        in_specs=[hbm, hbm, hbm, smem, smem],
        out_specs=(pl.BlockSpec(memory_space=pltpu.VMEM), pl.BlockSpec(memory_space=pltpu.VMEM)),
        scratch_shapes=[
            pltpu.VMEM((4, 2, 512, 512), F32),
            pltpu.VMEM((2, 512, 512), F32),
            pltpu.VMEM((2, 512, 512), F32),
            pltpu.VMEM((2, 512, 512), F32),
            pltpu.VMEM((4, 512, 512), F32),
            pltpu.VMEM((32, 8192), F32),
            pltpu.VMEM((32, 8192), F32),
            pltpu.VMEM((16, 32, 512), F32),
            pltpu.VMEM((512, 512), F32),
            pltpu.VMEM((512, 512), F32),
            pltpu.VMEM((16, 32, 512), F32),
            pltpu.VMEM((8, 8, 512), F32),
            pltpu.VMEM((8, 512), F32),
            dma((len(PIECES),)),
            dma((2,)),
            dma((n,)),
            dma((n,)),
            dma((8,)),
            dma((8,)),
            dma((16,)),
            dma((16,)),
            dma((16,)),
            dma((16,)),
        ],
        compiler_params=pltpu.CompilerParams(
            collective_id=0, has_side_effects=True, vmem_limit_bytes=48 << 20
        ),
        name="outer_step",
    )(local_params.reshape(4, 2, 512, 512), global_params, momentum, step_counts, alive)
    return out.reshape(4096, 512), nm


def solution(mesh):
    in_specs = (
        P("worker", None, "fsdp"),
        P(("worker", "fsdp"), None),
        P(("worker", "fsdp"), None),
        P("worker"),
        P("worker"),
    )
    out_specs = (P(None, "fsdp"), P(("worker", "fsdp"), None))
    return jax.shard_map(local, mesh=mesh, in_specs=in_specs, out_specs=out_specs, check_vma=False)
```

time: 309 us -> 138 us (0.45)
  waiting for transfers between devices: 221 us -> 0 us
  Pallas kernels: 0 us -> 131 us
  blocking collectives: 48.7 us -> 0 us
  between operations: 15.4 us -> 1.93 us
  other arithmetic: 9.84 us -> 0 us
  starting transfers between devices: 5.68 us -> 0 us
  local copies, waits for them, and re-layouts: 7.9 us -> 4.37 us
    pallas_call x0 -> x1, Pallas kernels: none -> 131 us  [local(): pl.pallas_call(kernel, out_shape=(pltpu.VMEM((4, 2, 512, 512), F32), pltp...]
    reduce_scatter x1 -> x0, waiting for transfers between devices: 117 us -> none  [local(): shared = lax.psum_scatter(term, 'worker', scatter_dimension=0, tiled=True)]
    all_gather x1 -> x0, waiting for transfers between devices: 104 us -> none  [local(): new_params = lax.all_gather(pieces, 'worker', axis=0, tiled=True)]
    all_to_all x1 -> x0, blocking collectives: 28.7 us -> none  [local(): lax.all_to_all(new_global, 'fsdp', split_axis=1, concat_axis=0, tiled=True)]
    psum x1 -> x0, blocking collectives: 19.9 us -> none  [local(): total = lax.psum(weight, 'worker')]
    mul x1 -> x0, other arithmetic: 7.81 us -> none  [local(): term = weight[0] * local_params[0]]
    all_to_all x1 -> x0, starting transfers between devices: 5.6 us -> none  [local(): lax.all_to_all(shared, 'fsdp', split_axis=0, concat_axis=1, tiled=True)]
    unnamed x5 -> x2, local copies, waits for them, and re-layouts: 7.76 us -> 4.37 us
  transfers between devices with their start and end apart: 3 -> 0, of which waited for: 2 -> 0; matrix products, arithmetic and copies ran while one was open for 0% -> 0% of each run, Pallas kernels for 0% -> 0%
where the time goes in v1:
time: 138 us
  Pallas kernels  131 us (95%)
  local copies, waits for them, and re-layouts  4.37 us (3%)
  between operations  1.93 us (1%)
    pallas_call x1, Pallas kernels, local(): pl.pallas_call(kernel, out_shape=(pltpu.VMEM((4, 2, 512, 512), F32), pltp...  131 us
    unnamed x2, local copies, waits for them, and re-layouts  4.37 us

profile of v1, /device:TPU:1, one launch (start us, length us, event | category | flops | bytes accessed | tf_op | source)
XLA Modules:
  0.0 137.8 jit_solution(876152413977785019)
XLA Ops:
  1.9 131.5 %outer_step.1 = (f32[4,2,512,512]{3,2,1,0:T(8,128)S(1)}, f32[32,8192]{1,0:T(8,128)S(1)}) custom-call(f32[4,2,512,512]{3,2,1,0:T(8,128)} %bitcast.3, f32[32,8192]{1,0:T(8,128)} %g_hbm.1, f32[32,8192]{1,0:T(8,128)} %m_hbm.1, s32[1]{0:T(128)S(6)} %copy.11.steps_ref, s32[1]{0:T(128)S(6)} %copy.12.alive_ref), custom_call_target="tpu_custom_call" | custom-call | tf_op jit(solution)/shard_map/outer_step/pallas_call | solution.py:317
  133.4 3.4 %copy.9 = f32[4096,512]{1,0:T(8,128)} copy(f32[4096,512]{1,0:T(8,128)S(1)} %bitcast.2) | data formatting | bytes 16777216
  136.8 1.0 copy.10

commit v2 on v1

v2 whole, which is shorter than its diff:
```python
import functools

import jax
import jax.numpy as jnp
from jax import lax
from jax.experimental import pallas as pl
from jax.experimental.pallas import tpu as pltpu
from jax.sharding import PartitionSpec as P

MESH = pl.DeviceIdType.MESH
F32 = jnp.float32

A = ((0, 4, 0, 16), (4, 4, 0, 16), (8, 4, 0, 16), (12, 4, 0, 16), (0, 8, 16, 8),)
B = ((8, 4, 16, 16), (12, 4, 16, 16), (0, 8, 24, 8),)
ORDER = [(c[0], c[1], int(c[2])) for c in (
    "LA0", "LB0", "LA1", "CA0", "FB0", "H00", "CA1", "LB1", "LA2", "CB0", "FB1", "CA2",
    "LB2", "LA3", "ZA0", "ZA1", "LA4", "CB1", "ZA2", "FB2", "CA3", "CA4", "NA0", "ZA3",
    "NA1", "NA2", "GA0", "ZA4", "CB2", "NA3", "GA1", "NB0", "GA2", "NB1", "NA4", "GA3",
    "U00", "XA0", "GB0", "XA1", "NB2", "GB1", "V00", "XA2", "GA4", "XA3", "XA4", "XB0",
    "PA0", "GB2", "XB1", "PA1", "PA2", "YB0", "PA3", "M00", "YB1", "YA0", "XB2", "YA1",
    "PA4", "EB0", "YA2", "EB1", "YA3", "EA0", "YB2", "EA1", "YA4", "EA2", "EB2", "EA3",
    "EA4",
)]


PIECES = {(kind, p): piece for kind, sizes in (("A", A), ("B", B)) for p, piece in enumerate(sizes)}


def part(key):
    f, nf, r, nr = PIECES[key]
    rows = pl.ds(r, nr)
    return (pl.ds(f, nf), rows), (pl.ds(f, nf // 2), rows), (pl.ds(f + nf // 2, nf // 2), rows)


LAG = 24
TAGS = {
    "A": ("fr", "fl", "cr", "cl", "z", "gz", "gr", "gl", "pr", "pl", "xr", "xl", "yr", "yl"),
    "B": ("zb0", "zb1", "zb2", "zb3", "fr", "fl", "cr", "cl", "gr", "gl", "xr", "xl", "gz0", "gz1", "gz2", "gz3"),
}
INDEX = {key: i for i, key in enumerate((t, k, p) for (k, p) in PIECES for t in TAGS[k])}


def kernel(
    local_ref, g_hbm, m_hbm, steps_hbm, alive_hbm, out, nm_out,
    work, rf, rcl, rcr, rz, g, m, hs, hr, hp, avr, wt, inv, scale, steps_ref, alive_ref,
    load_sem, gm_sem, send_sem, recv_sem, wt_send, wt_recv, h_send, h_recv, v_send, v_recv,
):
    w, f = lax.axis_index("worker"), lax.axis_index("fsdp")
    y, zh = w // 2, w % 2
    zo = 1 - zh
    yr, yl, y2 = (y + 1) % 4, (y + 3) % 4, (y + 2) % 4
    zl, fl = f // 8, f % 8

    def across(d):
        return y * 2 + zo, (1 - zl) * 8 + (fl + d) % 8

    right, left, over = (yr * 2 + zh, f), (yl * 2 + zh, f), (y * 2 + zo, f)

    def load(key):
        rows = part(key)[0]
        i = list(PIECES).index(key)
        return pltpu.make_async_copy(local_ref.at[:, :, *rows], work.at[:, :, *rows], load_sem.at[i])

    lorder = [(k, p) for s, k, p in ORDER if s == "L"]
    for key in lorder[:2]:
        load(key).start()
    steps_copy = pltpu.make_async_copy(steps_hbm, steps_ref, gm_sem.at[2])
    alive_copy = pltpu.make_async_copy(alive_hbm, alive_ref, gm_sem.at[3])
    steps_copy.start()
    alive_copy.start()
    g_copy = pltpu.make_async_copy(g_hbm, g, gm_sem.at[0])
    m_copy = pltpu.make_async_copy(m_hbm, m, gm_sem.at[1])

    barrier = pltpu.get_barrier_semaphore()

    def greet_worker(d, c):
        pl.semaphore_signal(barrier, inc=1, device_id=((w + d) % 8, f), device_id_type=MESH)
        return c

    def greet_fsdp(d, c):
        pl.semaphore_signal(barrier, inc=1, device_id=(w, (f + d) % 16), device_id_type=MESH)
        return c

    def greet_across(d, c):
        pl.semaphore_signal(barrier, inc=1, device_id=across(d), device_id_type=MESH)
        return c

    lax.fori_loop(1, 8, greet_worker, 0)
    lax.fori_loop(1, 16, greet_fsdp, 0)
    lax.fori_loop(0, 8, greet_across, 0)
    g_copy.start()
    m_copy.start()
    for key in lorder[2:]:
        load(key).start()
    steps_copy.wait()
    alive_copy.wait()

    weight = (steps_ref[0] * alive_ref[0]).astype(F32)

    def channel(tag, kind, p):
        rows, lo, hi = part((kind, p))
        if tag[:2] == "zb":
            t = {"0": y, "1": yr, "2": y2, "3": yl}[tag[2]]
            return work.at[t, zo, *rows], rz.at[t, *rows], over, rz.at[t, *rows]
        if tag == "z":
            return work.at[y, zo, *rows], rz.at[0, *rows], over, rz.at[0, *rows]
        if tag in ("fr", "fl", "cr", "cl"):
            z, q = (slice(None), slice(None)) if kind == "A" else (zh, 0)
            if tag == "fr":
                return work.at[y2, z, *lo], rf.at[q, *lo], right, rf.at[q, *lo]
            if tag == "fl":
                return work.at[y2, z, *hi], rf.at[q, *hi], left, rf.at[q, *hi]
            if tag == "cr":
                return work.at[yr, z, *rows], rcl.at[q, *rows], right, rcl.at[q, *rows]
            return work.at[yl, z, *rows], rcr.at[q, *rows], left, rcr.at[q, *rows]
        if tag[:2] == "gz":
            t = {"": y, "0": y, "1": yl, "2": y2, "3": yr}[tag[2:]]
            return out.at[t, zh, *rows], out.at[t, zh, *rows], over, out.at[t, zo, *rows]
        z = zo if tag[0] in "py" else zh
        if tag in ("gr", "pr"):
            return out.at[y, z, *rows], out.at[y, z, *rows], right, out.at[yl, z, *rows]
        if tag in ("gl", "pl"):
            return out.at[y, z, *rows], out.at[y, z, *rows], left, out.at[yr, z, *rows]
        if tag in ("xr", "yr"):
            return out.at[yl, z, *lo], out.at[yl, z, *lo], right, out.at[y2, z, *lo]
        return out.at[yr, z, *hi], out.at[yr, z, *hi], left, out.at[y2, z, *hi]

    sent = []

    def send(tag, kind, p):
        src, dst, device, _ = channel(tag, kind, p)
        i = INDEX[tag, kind, p]
        copy = pltpu.make_async_remote_copy(
            src, dst, send_sem.at[i], recv_sem.at[i], device_id=device, device_id_type=MESH
        )
        copy.start()
        sent.append((now, copy))

    def wait(tag, kind, p):
        src, _, device, land = channel(tag, kind, p)
        i = INDEX[tag, kind, p]
        pltpu.make_async_remote_copy(
            src, land, send_sem.at[i], recv_sem.at[i], device_id=device, device_id_type=MESH
        ).wait_recv()

    def weigh(key):
        rows = part(key)[0]
        load(key).wait()

        def body(i, c):
            ref = work.at[i // 2, i % 2, *rows]
            ref[...] = ref[...] * weight
            return c

        lax.fori_loop(0, 8, body, 0)

    def wt_copy(d):
        to, source = (w + d) % 8, (w + 8 - d) % 8
        return pltpu.make_async_remote_copy(
            wt.at[w], wt.at[w], wt_send.at[d], wt_recv.at[d], device_id=(to, f), device_id_type=MESH
        ), pltpu.make_async_remote_copy(
            wt.at[w], wt.at[source], wt_send.at[d], wt_recv.at[d], device_id=(to, f), device_id_type=MESH
        )

    def near(d):
        return zl * 8 + (fl + d) % 8, zl * 8 + (fl + 8 - d) % 8

    def cross(d):
        return (1 - zl) * 8 + (fl + d) % 8, (1 - zl) * 8 + (fl + 8 - d) % 8

    def both(src, dst, land, send, recv, i, device):
        return tuple(
            pltpu.make_async_remote_copy(
                src, t, send.at[i], recv.at[i], device_id=device, device_id_type=MESH
            )
            for t in (dst, land)
        )

    first, last = pl.ds(0, 16), pl.ds(16, 16)

    def h_near(d):
        to, source = near(d)
        return both(hs.at[to], hr.at[f], hr.at[source], h_send, h_recv, d, (w, to))

    def h_cross(d):
        to, source = cross(d)
        return both(
            hs.at[to, last], hr.at[f, last], hr.at[source, last], h_send, h_recv, 8 + d, (w, to)
        )

    def h_over(d):
        to, source = cross(d)
        return both(hs.at[to, first], hp.at[f], hp.at[source], h_send, h_recv, 16 + d, across(d))

    def v_near(d):
        to, source = near(d)
        return both(out.at[y, zh, to], avr.at[f], avr.at[source], v_send, v_recv, d, (w, to))

    def v_cross(d):
        to, source = cross(d)
        return both(
            out.at[y, zh, to, last], avr.at[f, last], avr.at[source, last],
            v_send, v_recv, 8 + d, (w, to),
        )

    def v_over(d):
        to, source = cross(d)
        return both(
            out.at[y, zo, to, first], avr.at[f, first], avr.at[source, first],
            v_send, v_recv, 16 + d, across(d),
        )

    def each(copies, n, what, first=1):
        def body(d, c):
            out_copy, in_copy = copies(d)
            if what == "start":
                out_copy.start()
            elif what == "recv":
                in_copy.wait_recv()
            else:
                out_copy.wait_send()
            return c

        lax.fori_loop(first, n, body, 0)

    ready = []

    def need_h():
        if ready:
            return
        ready.append(True)
        each(wt_copy, 8, "recv")
        total = wt[0]
        for i in range(1, 8):
            total = total + wt[i]
        inv[...] = 1.33 / total
        scale[...] = total / 1.33
        each(h_near, 8, "recv")
        each(h_cross, 8, "recv", 0)
        each(h_over, 8, "recv", 0)

    def finish(rows, s):
        out[y, zh, *rows] = s * inv[0:1, :] + hr[*rows]

    entered = []
    for now, (step, kind, p) in enumerate(ORDER):
        while sent and sent[0][0] < now - LAG:
            sent.pop(0)[1].wait_send()
        if step == "H":
            g_copy.wait()
            m_copy.wait()
            for i in range(16):
                cols = pl.ds(512 * i, 512)
                hs[i] = -0.33 * g[:, cols] - 0.567 * m[:, cols]
            hr[f] = hs[f]
            hr[pl.ds((1 - zl) * 8, 8), first] = jnp.zeros((8, 16, 512), F32)
            hp[pl.ds(zl * 8, 8)] = jnp.zeros((8, 16, 512), F32)
            each(h_cross, 8, "start", 0)
            each(h_over, 8, "start", 0)
            each(h_near, 8, "start")
            continue
        if step == "V":
            avr[f] = out[y, zh, f]
            each(v_cross, 8, "start", 0)
            each(v_near, 8, "start")
            continue
        if step == "U":
            each(v_over, 8, "start", 0)
            continue
        if step == "M":
            each(v_near, 8, "recv")
            each(v_cross, 8, "recv", 0)
            each(v_over, 8, "recv", 0)
            each(wt_copy, 8, "sent")
            for copies in (h_near, v_near):
                each(copies, 8, "sent")
            for copies in (h_cross, h_over, v_cross, v_over):
                each(copies, 8, "sent", 0)
            for i in range(16):
                cols = pl.ds(512 * i, 512)
                average = (avr[i] + 0.33 * g[:, cols] + 0.567 * m[:, cols]) * (1 / 1.33)
                nm_out[:, cols] = 0.9 * m[:, cols] + (g[:, cols] - average)
            continue
        rows, lo, hi = part((kind, p))
        if step == "L":
            weigh((kind, p))
            if not entered:
                entered.append(True)
                wt[w] = jnp.full((8, 512), weight, F32)
                pl.semaphore_wait(barrier, 30)
                each(wt_copy, 8, "start")
            for tag in ("fr", "fl") if kind == "A" else ("zb2", "zb1", "zb3", "zb0"):
                send(tag, kind, p)
        elif step == "F":
            wait("zb2", kind, p)
            work[y2, zh, *rows] += rz[y2, *rows]
            send("fr", kind, p)
            send("fl", kind, p)
        elif step == "C":
            wait("fr", kind, p)
            wait("fl", kind, p)
            if kind == "A":
                for z in range(2):
                    work[yr, z, *lo] += rf[z, *lo]
                    work[yl, z, *hi] += rf[z, *hi]
            else:
                wait("zb1", kind, p)
                wait("zb3", kind, p)
                work[yr, zh, *lo] += rz[yr, *lo] + rf[0, *lo]
                work[yr, zh, *hi] += rz[yr, *hi]
                work[yl, zh, *lo] += rz[yl, *lo]
                work[yl, zh, *hi] += rz[yl, *hi] + rf[0, *hi]
            send("cr", kind, p)
            send("cl", kind, p)
        elif step == "Z":
            wait("cr", kind, p)
            wait("cl", kind, p)
            for z in range(2):
                work[y, z, *rows] += rcl[z, *rows] + rcr[z, *rows]
            fs, fn, r, _ = PIECES[kind, p]
            if r < 16:
                need_h()
                work[y, zo, *rows] += hp[fs : fs + fn] * scale[0:1, :]
            send("z", kind, p)
        elif step == "N":
            if kind == "A":
                wait("z", kind, p)
                need_h()
                finish(rows, work[y, zh, *rows] + rz[0, *rows])
                for tag in ("gz", "gr", "gl"):
                    send(tag, kind, p)
            else:
                wait("cr", kind, p)
                wait("cl", kind, p)
                wait("zb0", kind, p)
                need_h()
                finish(rows, work[y, zh, *rows] + rz[y, *rows] + rcl[0, *rows] + rcr[0, *rows])
                for tag in ("gr", "gl", "gz0"):
                    send(tag, kind, p)
        elif step == "P":
            send("pr", kind, p)
            send("pl", kind, p)
        elif step == "X":
            wait("gr", kind, p)
            wait("gl", kind, p)
            send("xr", kind, p)
            send("xl", kind, p)
            if kind == "B":
                send("gz1", kind, p)
                send("gz3", kind, p)
        elif step == "Y":
            if kind == "A":
                wait("pr", kind, p)
                wait("pl", kind, p)
                send("yr", kind, p)
                send("yl", kind, p)
            else:
                wait("xr", kind, p)
                wait("xl", kind, p)
                send("gz2", kind, p)
        elif step == "G":
            wait("gz0" if kind == "B" else "gz", kind, p)
        elif step == "E":
            for tag in ("xr", "xl", "yr", "yl") if kind == "A" else ("gz1", "gz3", "gz2"):
                wait(tag, kind, p)

    for _, copy in sent:
        copy.wait_send()


def store(a_ref, b_ref, a_out, b_out, sem):
    copies = [pltpu.make_async_copy(a_ref.at[i // 2, i % 2], a_out.at[i // 2, i % 2], sem.at[i]) for i in range(8)]
    copies.append(pltpu.make_async_copy(b_ref, b_out, sem.at[8]))
    for copy in copies:
        copy.start()
    for copy in copies:
        copy.wait()


def local(local_params, global_params, momentum, step_counts, alive):
    hbm = pl.BlockSpec(memory_space=pltpu.HBM)
    n = len(INDEX)
    dma = pltpu.SemaphoreType.DMA
    out, nm = pl.pallas_call(
        kernel,
        out_shape=(pltpu.VMEM((4, 2, 16, 32, 512), F32), pltpu.VMEM((32, 8192), F32)),
        in_specs=[hbm] * 5,
        out_specs=(pl.BlockSpec(memory_space=pltpu.VMEM), pl.BlockSpec(memory_space=pltpu.VMEM)),
        scratch_shapes=[
            pltpu.VMEM((4, 2, 16, 32, 512), F32),
            pltpu.VMEM((2, 16, 32, 512), F32),
            pltpu.VMEM((2, 16, 32, 512), F32),
            pltpu.VMEM((2, 16, 32, 512), F32),
            pltpu.VMEM((4, 16, 32, 512), F32),
            pltpu.VMEM((32, 8192), F32),
            pltpu.VMEM((32, 8192), F32),
            pltpu.VMEM((16, 32, 512), F32),
            pltpu.VMEM((16, 32, 512), F32),
            pltpu.VMEM((16, 16, 512), F32),
            pltpu.VMEM((16, 32, 512), F32),
            pltpu.VMEM((8, 8, 512), F32),
            pltpu.VMEM((8, 512), F32),
            pltpu.VMEM((8, 512), F32),
            pltpu.SMEM((1,), jnp.int32),
            pltpu.SMEM((1,), jnp.int32),
            dma((len(PIECES),)),
            dma((4,)),
            dma((n,)),
            dma((n,)),
            dma((8,)),
            dma((8,)),
            dma((24,)),
            dma((24,)),
            dma((24,)),
            dma((24,)),
        ],
        compiler_params=pltpu.CompilerParams(
            collective_id=0, has_side_effects=True, vmem_limit_bytes=48 << 20
        ),
        name="outer_step",
    )(local_params.reshape(4, 2, 16, 32, 512), global_params, momentum, step_counts, alive)
    out, nm = pl.pallas_call(
        store,
        out_shape=(jax.ShapeDtypeStruct((4, 2, 16, 32, 512), F32), jax.ShapeDtypeStruct((32, 8192), F32)),
        in_specs=[pl.BlockSpec(memory_space=pltpu.VMEM)] * 2,
        out_specs=(hbm, hbm),
        scratch_shapes=[dma((9,))],
        compiler_params=pltpu.CompilerParams(vmem_limit_bytes=16 << 20),
        name="store",
    )(out, nm)
    return out.reshape(4096, 512), nm


def solution(mesh):
    in_specs = (
        P("worker", None, "fsdp"),
        P(("worker", "fsdp"), None),
        P(("worker", "fsdp"), None),
        P("worker"),
        P("worker"),
    )
    out_specs = (P(None, "fsdp"), P(("worker", "fsdp"), None))
    return jax.shard_map(local, mesh=mesh, in_specs=in_specs, out_specs=out_specs, check_vma=False)
```

time: 138 us -> 133 us (0.964)
  local copies, waits for them, and re-layouts: 4.37 us -> 0 us
    unnamed x2 -> x0, local copies, waits for them, and re-layouts: 4.37 us -> none
    pallas_call x1 -> x2, Pallas kernels: 131 us -> 130 us  [the longest x1 126 us: local(): pl.pallas_call(kernel, out_shape=(pltpu.VMEM((4, 2, 16, 32, 512), F32), p...]
where the time goes in v2:
time: 133 us; the launch traced here: 132 us
  Pallas kernels  130 us (98%)
  between operations  1.93 us (1%)
    pallas_call x1, Pallas kernels, local(): pl.pallas_call(kernel, out_shape=(pltpu.VMEM((4, 2, 16, 32, 512), F32), p...  126 us
    pallas_call x1, Pallas kernels, local(): pl.pallas_call(store, out_shape=(jax.ShapeDtypeStruct((4, 2, 16, 32, 512)...  3.69 us

profile of v2, /device:TPU:1, one launch (start us, length us, event | category | flops | bytes accessed | tf_op | source)
XLA Modules:
  0.0 131.7 jit_solution(12742273035941118056)
XLA Ops:
  1.9 126.1 %outer_step.1 = (f32[4,2,16,32,512]{4,3,2,1,0:T(8,128)S(1)}, f32[32,8192]{1,0:T(8,128)S(1)}) custom-call(f32[4,2,16,32,512]{4,3,2,1,0:T(8,128)} %bitcast.2, f32[32,8192]{1,0:T(8,128)} %g_hbm.1, f32[32,8192]{1,0:T(8,128)} %m_hbm.1, s32[1]{0:T(128)S(6)} %copy.7.steps_hbm, s32[1]{0:T(128)S(6)} %copy.8.alive_hbm), custom_call_target="tpu_custom_call" | custom-call | tf_op jit(solution)/shard_map/outer_step/pallas_call | solution.py:384
  128.0 3.7 %store.1 = (f32[4,2,16,32,512]{4,3,2,1,0:T(8,128)}, f32[32,8192]{1,0:T(8,128)}) custom-call(f32[4,2,16,32,512]{4,3,2,1,0:T(8,128)S(1)} %get-tuple-element.6.a_ref, f32[32,8192]{1,0:T(8,128)S(1)} %get-tuple-element.7.b_ref), custom_call_target="tpu_custom_call" | custom-call | tf_op jit(solution)/shard_map/store/pallas_call | solution.py:422

commit v3 on v2

--- a/solution.py
+++ b/solution.py
@@ -10,15 +10,15 @@
 MESH = pl.DeviceIdType.MESH
 F32 = jnp.float32
 
-A = ((0, 4, 0, 16), (4, 4, 0, 16), (8, 4, 0, 16), (12, 4, 0, 16), (0, 8, 16, 8),)
-B = ((8, 4, 16, 16), (12, 4, 16, 16), (0, 8, 24, 8),)
+A = ((0, 4, 0, 16), (4, 4, 0, 16), (8, 4, 0, 16), (12, 4, 0, 16), (0, 4, 16, 16),)
+B = ((4, 4, 16, 16), (8, 4, 16, 16), (12, 4, 16, 16),)
 ORDER = [(c[0], c[1], int(c[2])) for c in (
-    "LA0", "LB0", "LA1", "CA0", "FB0", "H00", "CA1", "LB1", "LA2", "CB0", "FB1", "CA2",
-    "LB2", "LA3", "ZA0", "ZA1", "LA4", "CB1", "ZA2", "FB2", "CA3", "CA4", "NA0", "ZA3",
-    "NA1", "NA2", "GA0", "ZA4", "CB2", "NA3", "GA1", "NB0", "GA2", "NB1", "NA4", "GA3",
-    "U00", "XA0", "GB0", "XA1", "NB2", "GB1", "V00", "XA2", "GA4", "XA3", "XA4", "XB0",
-    "PA0", "GB2", "XB1", "PA1", "PA2", "YB0", "PA3", "M00", "YB1", "YA0", "XB2", "YA1",
-    "PA4", "EB0", "YA2", "EB1", "YA3", "EA0", "YB2", "EA1", "YA4", "EA2", "EB2", "EA3",
+    "LA0", "H00", "LA1", "LA2", "LB0", "LA3", "CA0", "CA1", "LB1", "CA2", "ZA0", "CA3",
+    "LB2", "ZA1", "LA4", "FB0", "FB1", "ZA2", "ZA3", "FB2", "CA4", "CB0", "CB1", "CB2",
+    "NA0", "ZA4", "NA1", "NA2", "NA3", "GA0", "PA0", "NA4", "GA1", "NB0", "GA2", "NB1",
+    "GA3", "U00", "XA0", "NB2", "GA4", "V00", "XA1", "GB0", "XA2", "XA3", "GB1", "XB0",
+    "XA4", "YA0", "XB1", "GB2", "PA1", "PA2", "XB2", "PA3", "EA0", "YB0", "M00", "PA4",
+    "YB1", "YA1", "YA2", "YB2", "YA3", "EB0", "YA4", "EA1", "EB1", "EA2", "EA3", "EB2",
     "EA4",
 )]
 
@@ -255,6 +255,7 @@
             hr[f] = hs[f]
             hr[pl.ds((1 - zl) * 8, 8), first] = jnp.zeros((8, 16, 512), F32)
             hp[pl.ds(zl * 8, 8)] = jnp.zeros((8, 16, 512), F32)
+            each(wt_copy, 8, "start")
             each(h_cross, 8, "start", 0)
             each(h_over, 8, "start", 0)
             each(h_near, 8, "start")
@@ -288,7 +289,6 @@
                 entered.append(True)
                 wt[w] = jnp.full((8, 512), weight, F32)
                 pl.semaphore_wait(barrier, 30)
-                each(wt_copy, 8, "start")
             for tag in ("fr", "fl") if kind == "A" else ("zb2", "zb1", "zb3", "zb0"):
                 send(tag, kind, p)
         elif step == "F":

time: 133 us -> 132 us (level)
  no operation moved by 1% of the time
where the time goes in v3:
time: 132 us
  Pallas kernels  130 us (98%)
  between operations  1.93 us (1%)
    pallas_call x1, Pallas kernels, local(): pl.pallas_call(kernel, out_shape=(pltpu.VMEM((4, 2, 16, 32, 512), F32), p...  126 us
    pallas_call x1, Pallas kernels, local(): pl.pallas_call(store, out_shape=(jax.ShapeDtypeStruct((4, 2, 16, 32, 512)...  3.69 us

profile of v3, /device:TPU:1, one launch (start us, length us, event | category | flops | bytes accessed | tf_op | source)
XLA Modules:
  0.0 131.6 jit_solution(7266797135822003533)
XLA Ops:
  1.9 125.9 %outer_step.1 = (f32[4,2,16,32,512]{4,3,2,1,0:T(8,128)S(1)}, f32[32,8192]{1,0:T(8,128)S(1)}) custom-call(f32[4,2,16,32,512]{4,3,2,1,0:T(8,128)} %bitcast.2, f32[32,8192]{1,0:T(8,128)} %g_hbm.1, f32[32,8192]{1,0:T(8,128)} %m_hbm.1, s32[1]{0:T(128)S(6)} %copy.7.steps_hbm, s32[1]{0:T(128)S(6)} %copy.8.alive_hbm), custom_call_target="tpu_custom_call" | custom-call | tf_op jit(solution)/shard_map/outer_step/pallas_call | solution.py:384
  127.9 3.7 %store.1 = (f32[4,2,16,32,512]{4,3,2,1,0:T(8,128)}, f32[32,8192]{1,0:T(8,128)}) custom-call(f32[4,2,16,32,512]{4,3,2,1,0:T(8,128)S(1)} %get-tuple-element.6.a_ref, f32[32,8192]{1,0:T(8,128)S(1)} %get-tuple-element.7.b_ref), custom_call_target="tpu_custom_call" | custom-call | tf_op jit(solution)/shard_map/store/pallas_call | solution.py:422

commit v4 on v3

--- a/solution.py
+++ b/solution.py
@@ -10,16 +10,13 @@
 MESH = pl.DeviceIdType.MESH
 F32 = jnp.float32
 
-A = ((0, 4, 0, 16), (4, 4, 0, 16), (8, 4, 0, 16), (12, 4, 0, 16), (0, 4, 16, 16),)
-B = ((4, 4, 16, 16), (8, 4, 16, 16), (12, 4, 16, 16),)
+A = ((0, 8, 0, 16), (8, 8, 0, 16), (0, 4, 16, 16),)
+B = ((4, 4, 16, 16), (8, 8, 16, 16),)
 ORDER = [(c[0], c[1], int(c[2])) for c in (
-    "LA0", "H00", "LA1", "LA2", "LB0", "LA3", "CA0", "CA1", "LB1", "CA2", "ZA0", "CA3",
-    "LB2", "ZA1", "LA4", "FB0", "FB1", "ZA2", "ZA3", "FB2", "CA4", "CB0", "CB1", "CB2",
-    "NA0", "ZA4", "NA1", "NA2", "NA3", "GA0", "PA0", "NA4", "GA1", "NB0", "GA2", "NB1",
-    "GA3", "U00", "XA0", "NB2", "GA4", "V00", "XA1", "GB0", "XA2", "XA3", "GB1", "XB0",
-    "XA4", "YA0", "XB1", "GB2", "PA1", "PA2", "XB2", "PA3", "EA0", "YB0", "M00", "PA4",
-    "YB1", "YA1", "YA2", "YB2", "YA3", "EB0", "YA4", "EA1", "EB1", "EA2", "EA3", "EB2",
-    "EA4",
+    "LA0", "LA1", "H00", "LA2", "LB0", "CA0", "LB1", "FB0", "CA1", "ZA0", "FB1", "CB0",
+    "CA2", "ZA1", "CB1", "NA0", "ZA2", "NA1", "GA0", "PA0", "NA2", "GA1", "U00", "NB0",
+    "GA2", "NB1", "V00", "GB0", "YA0", "XB0", "XA0", "GB1", "XA1", "XB1", "XA2", "PA1",
+    "EA0", "M00", "YB0", "PA2", "YB1", "YA1", "EB0", "YA2", "EA1", "EB1", "EA2",
 )]
 
 

time: 132 us -> 131 us (level)
  no operation moved by 1% of the time
where the time goes in v4:
time: 131 us
  Pallas kernels  129 us (98%)
  between operations  1.93 us (1%)
    pallas_call x1, Pallas kernels, local(): pl.pallas_call(kernel, out_shape=(pltpu.VMEM((4, 2, 16, 32, 512), F32), p...  125 us
    pallas_call x1, Pallas kernels, local(): pl.pallas_call(store, out_shape=(jax.ShapeDtypeStruct((4, 2, 16, 32, 512)...  3.69 us

profile of v4, /device:TPU:1, one launch (start us, length us, event | category | flops | bytes accessed | tf_op | source)
XLA Modules:
  0.0 130.7 jit_solution(8592830018211290767)
XLA Ops:
  1.9 125.1 %outer_step.1 = (f32[4,2,16,32,512]{4,3,2,1,0:T(8,128)S(1)}, f32[32,8192]{1,0:T(8,128)S(1)}) custom-call(f32[4,2,16,32,512]{4,3,2,1,0:T(8,128)} %bitcast.2, f32[32,8192]{1,0:T(8,128)} %g_hbm.1, f32[32,8192]{1,0:T(8,128)} %m_hbm.1, s32[1]{0:T(128)S(6)} %copy.7.steps_hbm, s32[1]{0:T(128)S(6)} %copy.8.alive_hbm), custom_call_target="tpu_custom_call" | custom-call | tf_op jit(solution)/shard_map/outer_step/pallas_call | solution.py:381
  127.1 3.7 %store.1 = (f32[4,2,16,32,512]{4,3,2,1,0:T(8,128)}, f32[32,8192]{1,0:T(8,128)}) custom-call(f32[4,2,16,32,512]{4,3,2,1,0:T(8,128)S(1)} %get-tuple-element.6.a_ref, f32[32,8192]{1,0:T(8,128)S(1)} %get-tuple-element.7.b_ref), custom_call_target="tpu_custom_call" | custom-call | tf_op jit(solution)/shard_map/store/pallas_call | solution.py:419

commit v5 on v4

--- a/solution.py
+++ b/solution.py
@@ -14,9 +14,9 @@
 B = ((4, 4, 16, 16), (8, 8, 16, 16),)
 ORDER = [(c[0], c[1], int(c[2])) for c in (
     "LA0", "LA1", "H00", "LA2", "LB0", "CA0", "LB1", "FB0", "CA1", "ZA0", "FB1", "CB0",
-    "CA2", "ZA1", "CB1", "NA0", "ZA2", "NA1", "GA0", "PA0", "NA2", "GA1", "U00", "NB0",
-    "GA2", "NB1", "V00", "GB0", "YA0", "XB0", "XA0", "GB1", "XA1", "XB1", "XA2", "PA1",
-    "EA0", "M00", "YB0", "PA2", "YB1", "YA1", "EB0", "YA2", "EA1", "EB1", "EA2",
+    "CA2", "ZA1", "CB1", "NB0", "ZA2", "NA0", "GB0", "NB1", "NA1", "GA0", "XA0", "GB1",
+    "NA2", "V00", "PA0", "GA1", "U00", "GA2", "XB0", "XA1", "XB1", "XA2", "YA0", "PA1",
+    "M00", "YB0", "PA2", "YB1", "EA0", "YA1", "EB0", "YA2", "EA1", "EB1", "EA2",
 )]
 
 

time: 131 us -> 136 us (1.038)
  Pallas kernels: 129 us -> 134 us
    pallas_call x1, Pallas kernels: 125 us -> 130 us  [local(): pl.pallas_call(kernel, out_shape=(pltpu.VMEM((4, 2, 16, 32, 512), F32), p...]
where the time goes in v5:
time: 136 us
  Pallas kernels  134 us (99%)
  between operations  1.93 us (1%)
    pallas_call x1, Pallas kernels, local(): pl.pallas_call(kernel, out_shape=(pltpu.VMEM((4, 2, 16, 32, 512), F32), p...  130 us
    pallas_call x1, Pallas kernels, local(): pl.pallas_call(store, out_shape=(jax.ShapeDtypeStruct((4, 2, 16, 32, 512)...  3.69 us

profile of v5, /device:TPU:1, one launch (start us, length us, event | category | flops | bytes accessed | tf_op | source)
XLA Modules:
  0.0 136.0 jit_solution(9820549630939139664)
XLA Ops:
  1.9 130.4 %outer_step.1 = (f32[4,2,16,32,512]{4,3,2,1,0:T(8,128)S(1)}, f32[32,8192]{1,0:T(8,128)S(1)}) custom-call(f32[4,2,16,32,512]{4,3,2,1,0:T(8,128)} %bitcast.2, f32[32,8192]{1,0:T(8,128)} %g_hbm.1, f32[32,8192]{1,0:T(8,128)} %m_hbm.1, s32[1]{0:T(128)S(6)} %copy.7.steps_hbm, s32[1]{0:T(128)S(6)} %copy.8.alive_hbm), custom_call_target="tpu_custom_call" | custom-call | tf_op jit(solution)/shard_map/outer_step/pallas_call | solution.py:381
  132.3 3.7 %store.1 = (f32[4,2,16,32,512]{4,3,2,1,0:T(8,128)}, f32[32,8192]{1,0:T(8,128)}) custom-call(f32[4,2,16,32,512]{4,3,2,1,0:T(8,128)S(1)} %get-tuple-element.6.a_ref, f32[32,8192]{1,0:T(8,128)S(1)} %get-tuple-element.7.b_ref), custom_call_target="tpu_custom_call" | custom-call | tf_op jit(solution)/shard_map/store/pallas_call | solution.py:419
